TPU v7x, 32 devices: a whole 2x2x4 slice. The times are simulated.
32 devices in a mesh: parts: 2 (over y), chan: 16 (over z, x, core).
Axes of the slice: x: 2, y: 2, z: 4, core: 2. Of those that a mesh axis runs over, the one named last changes fastest.
Arguments:
- samples: bfloat16 [4096, 16, 512], P(('parts', 'chan')), parts along dimension 0, may hold values from -160 to 160
- pair_blocks: int32 [32, 2], P('parts'), parts along dimension 0, may hold values from 0 to 15, as said below
Outputs:
- cross: bfloat16 [32, 128, 2, 128, 128], P(('parts', 'chan')), parts along dimension 0
There are 2 independent parts, one for each index of `parts`. A program takes and returns all parts, laid end to end along the dimension named above; each array names one. Nothing has to cross between parts.
Inputs may be any that keep to these rules, and one draw needn't show every extreme that they name: `pair_blocks`: each row names two channel blocks, the first no greater than the second and at most 4 blocks before it; no two rows are equal.
All inputs are finite; a program needn't handle non-finite values.
Results may differ from a plain program's by a relative error of at most 0.0064.
Values may be sent and summed in bfloat16 or wider, within the bound.
A program may use at most 128 MiB of HBM per device.

v0:
```python
import math

import jax
import jax.numpy as jnp
from jax import lax
from jax.sharding import PartitionSpec as P

FREQS = 128
BLOCK = 128
SMOOTH = 4


def fourier_table(bins, length):
    positions = jnp.arange(length, dtype=jnp.int32)
    numbers = jnp.arange(1, bins + 1, dtype=jnp.int32)
    turns = (numbers[:, None] * positions[None, :] % length).astype(jnp.float32)
    phase = 2.0 * math.pi * turns / length
    taper = 0.5 - 0.5 * jnp.cos(2.0 * math.pi * positions.astype(jnp.float32) / length)
    table = jnp.stack([taper[None, :] * jnp.cos(phase), -taper[None, :] * jnp.sin(phase)], axis=1)
    return table.astype(jnp.bfloat16)


def band_matrix(bins):
    index = jnp.arange(bins, dtype=jnp.int32)
    near = (jnp.abs(index[:, None] - index[None, :]) <= SMOOTH).astype(jnp.float32)
    return near / jnp.sum(near, axis=1, keepdims=True)


def whiten(spectra, common, band):
    demeaned = spectra - common[..., None]
    amplitude = jnp.sqrt(demeaned[:, :, 0, :] ** 2 + demeaned[:, :, 1, :] ** 2)
    smoothed = jnp.einsum("fg,gwc->fwc", band, amplitude, precision=lax.Precision.HIGHEST)
    level = jnp.mean(amplitude, axis=0)
    denominator = smoothed + 0.05 * level[None] + 1e-06
    return (demeaned / denominator[:, :, None, :]).astype(jnp.bfloat16)


def block_slice(spectra, block_index):
    piece = lax.dynamic_slice_in_dim(spectra, block_index * BLOCK, BLOCK, 3)
    return piece.reshape(piece.shape[0], piece.shape[1], 2 * BLOCK)


def cross_spectrum(first, second, scale):
    width = first.shape[2] // 2
    product = lax.dot_general(
        first, second, (((1,), (1,)), ((0,), (0,))), preferred_element_type=jnp.float32
    )
    real_part = product[:, :width, :width] + product[:, width:, width:]
    imag_part = product[:, width:, :width] - product[:, :width, width:]
    return (jnp.stack([real_part, imag_part], axis=1) * scale).astype(jnp.bfloat16)


def shards(samples, pair_blocks):
    ch_local, windows, length = samples.shape
    devices = lax.axis_size("chan")
    table = fourier_table(FREQS, length)
    spectra = jnp.einsum("fkl,cwl->fwkc", table, samples, preferred_element_type=jnp.float32)
    total = lax.psum(jnp.sum(spectra, axis=3), "chan")
    common = total / (ch_local * devices)
    whitened = whiten(spectra, common, band_matrix(FREQS))
    by_bins = lax.all_to_all(whitened, "chan", split_axis=0, concat_axis=3, tiled=True)
    scale = 1.0 / math.sqrt(windows)

    def both_blocks(pair):
        return jnp.concatenate(
            [block_slice(by_bins, pair[0]), block_slice(by_bins, pair[1])], axis=2
        )

    stacked = lax.map(both_blocks, pair_blocks)
    owned = lax.all_to_all(stacked, "chan", split_axis=0, concat_axis=1, tiled=True)
    middle = owned.shape[3] // 2
    return cross_spectrum(owned[0, :, :, :middle], owned[0, :, :, middle:], scale)[None]


def solution(mesh):
    placed = (P(("parts", "chan"), None, None), P("parts", None))
    return jax.shard_map(
        shards,
        mesh=mesh,
        in_specs=placed,
        out_specs=P(("parts", "chan"), None, None, None, None),
        check_vma=False,
    )
```

profile of v0, /device:TPU:27, one launch (start us, length us, event | category | flops | bytes accessed | tf_op | source)
XLA Modules:
  0.0 251.2 jit_solution(4912483341813186456)
XLA Ops:
  0.2 1.3 multiply_convert_fusion.1
  1.4 4.4 %bitcast_reduce_fusion = (f32[128,16,2]{0,1,2:T(8,128)S(1)}, f32[128,2,128,16]{2,0,3,1:T(8,128)S(1)}) fusion(bf16[128,16,512]{2,1,0:T(8,128)(2,1)} %param.4, bf16[128,1,512]{2,0,1:T(8,128)(2,1)S(1)} %get-tuple-element.43, bf16[128,1,512]{2,0,1:T(8,128)(2,1)S(1)} %get-tuple-element.42), kind=kOutput, calls=%fused_computation.12 | convolution fusion | flops 537915392 | bytes 4472832 | tf_op jit(solution)/shard_map/fkl,cwl->fwkc/dot_general | solution.py:57
  5.8 57.0 %psum.7 = f32[128,16,2]{0,1,2:T(8,128)S(1)} all-reduce(f32[128,16,2]{0,1,2:T(8,128)S(1)} %get-tuple-element.44), channel_id=1, replica_groups=mesh['parts'=2,'chan'=16] {'chan'}, use_global_device_ids=true, to_apply=%region_1.2 | all-reduce | flops 4096 | bytes 32768 | tf_op jit(solution)/shard_map/psum | solution.py:58
  62.8 0.6 bitcast_subtract_fusion
  63.8 1.4 fusion.7
  65.2 0.7 divide_convert_fusion
  65.9 1.7 copy.7
  67.6 8.5 %all-to-all-start = ((bf16[128,16,2,128]{3,1,2,0:T(8,128)(2,1)}), bf16[128,16,2,128]{3,1,2,0:T(8,128)(2,1)S(1)}, u32[]{:S(2)}, u32[]{:S(2)}) async-start(bf16[128,16,2,128]{3,1,2,0:T(8,128)(2,1)} %copy.7), calls=%async_computation | async-start | bytes 2097152 | tf_op jit(solution)/shard_map/all_to_all | solution.py:61
  76.1 23.9 %all-to-all-done = bf16[128,16,2,128]{3,1,2,0:T(8,128)(2,1)S(1)} async-done(((bf16[128,16,2,128]{3,1,2,0:T(8,128)(2,1)}), bf16[128,16,2,128]{3,1,2,0:T(8,128)(2,1)S(1)}, u32[]{:S(2)}, u32[]{:S(2)}) %all-to-all-start) | async-done | bytes 1048608 | tf_op jit(solution)/shard_map/all_to_all | solution.py:61
  100.0 0.7 copy.8
  101.0 45.1 %while.10 = (s32[]{:T(128)}, bf16[16,8,16,512]{3,2,1,0:T(8,128)(2,1)}, s32[16,2]{0,1:T(2,128)S(1)}, bf16[8,16,2,2048]{3,2,1,0:T(2,128)(2,1)S(1)}, s32[]{:T(128)}, /*index=5*/s32[1,1]{0,1:T(1,128)}, s32[]{:T(128)}, s32[]{:T(128)}) while((s32[]{:T(128)}, bf16[16,8,16,512]{3,2,1,0:T(8,128)(2,1)}, s32[16,2]{0,1:T(2,128)S(1)}, ...), condition=%wide.region_5.6_spmd, body=%wide.region_4.5_spmd.sunk | while | flops 262154 | bytes 786665 | solution.py:69
  103.2 0.7 fusion.33
  106.0 0.7 fusion.33
  108.8 0.7 fusion.33
  111.6 0.7 fusion.33
  114.5 0.7 fusion.33
  117.3 0.7 fusion.33
  120.1 0.7 fusion.33
  122.9 0.7 fusion.33
  125.7 0.7 fusion.33
  128.6 0.7 fusion.33
  131.4 0.7 fusion.33
  134.2 0.7 fusion.33
  137.0 0.7 fusion.33
  139.8 0.7 fusion.33
  142.7 0.7 fusion.33
  145.5 0.7 fusion.33
  146.2 52.4 %all_to_all.30 = bf16[16,8,16,512]{3,2,1,0:T(8,128)(2,1)S(1)} all-to-all(bf16[16,8,16,512]{3,2,1,0:T(8,128)(2,1)} %get-tuple-element.27), channel_id=1, replica_groups=mesh['parts'=2,'chan'=16] {'chan'}, dimensions={0} | all-to-all | bytes 4194304 | tf_op jit(solution)/shard_map/all_to_all | solution.py:70
  198.6 13.1 %fusion.8 = f32[128,256,256]{2,1,0:T(8,128)} fusion(bf16[1,128,16,512]{3,2,1,0:T(8,128)(2,1)S(1)} %bitcast.51), kind=kOutput, calls=%fused_computation.20 | convolution fusion | flops 268435456 | bytes 35651584 | tf_op jit(solution)/shard_map/dot_general | solution.py:45
  211.7 19.5 %fusion.3 = (f32[1,128,1,128,128]{4,3,1,2,0:T(8,128)}, f32[1,128,1,128,128]{4,3,1,2,0:T(8,128)}) fusion(f32[128,256,256]{2,1,0:T(8,128)} %fusion.8), kind=kLoop, calls=%fused_computation.10 | loop fusion | flops 4194304 | bytes 50331648 | tf_op jit(solution)/shard_map/stack | solution.py:50
  231.2 9.5 %fusion.1 = bf16[1,128,2,128,128]{4,3,1,2,0:T(8,128)(2,1)} fusion(f32[1,128,1,128,128]{4,3,1,2,0:T(8,128)} %get-tuple-element.41, f32[1,128,1,128,128]{4,3,1,2,0:T(8,128)} %get-tuple-element.40), kind=kLoop, calls=%fused_computation.6 | loop fusion | flops 12582912 | bytes 25165824 | tf_op jit(solution)/shard_map/convert_element_type | solution.py:50
  240.7 10.5 %copy.9 = bf16[1,128,2,128,128]{4,3,2,1,0:T(8,128)(2,1)} copy(bf16[1,128,2,128,128]{4,3,1,2,0:T(8,128)(2,1)} %fusion.1) | data formatting | bytes 16777216 | tf_op jit(solution)/shard_map/convert_element_type | solution.py:50
  (90 shorter events, 14.7 us)
Async XLA Ops:
  67.6 32.4 %all-to-all-start = ((bf16[128,16,2,128]{3,1,2,0:T(8,128)(2,1)}), bf16[128,16,2,128]{3,1,2,0:T(8,128)(2,1)S(1)}, u32[]{:S(2)}, u32[]{:S(2)}) async-start(bf16[128,16,2,128]{3,1,2,0:T(8,128)(2,1)} %copy.7), calls=%async_computation | async-start | bytes 2097152 | tf_op jit(solution)/shard_map/all_to_all | solution.py:61
  100.0 1.0 copy-start
where the time goes:
time: 254 us; the launch traced here: 251 us
  blocking collectives  109 us (43%)
  other arithmetic  42.9 us (17%)
  local copies, waits for them, and re-layouts  27 us (11%)
  waiting for transfers between devices  23.9 us (9%)
  loops' own time  20.6 us (8%)
  matrix products  18.8 us (7%)
  starting transfers between devices  8.54 us (3%)
    psum x1, blocking collectives, shards(): total = lax.psum(jnp.sum(spectra, axis=3), 'chan')  57 us
    all_to_all x1, blocking collectives, shards(): lax.all_to_all(stacked, 'chan', split_axis=0, concat_axis=1, tiled=True)  52.4 us
    all_to_all x1, waiting for transfers between devices, shards(): lax.all_to_all(whitened, 'chan', split_axis=0, concat_axis=3, tiled=True)  23.9 us
    another operation x1, loops' own time, shards(): stacked = lax.map(both_blocks, pair_blocks)  20.6 us
    another operation x1, other arithmetic, cross_spectrum(): jnp.stack([real_part, imag_part], axis=1) * scale  19.5 us
    dot_general x1, matrix products, cross_spectrum(): lax.dot_general(first, second, (((1,), (1,)), ((0,), (0,))), preferred_el...  13.1 us
    dynamic_update_slice x16, other arithmetic, shards(): stacked = lax.map(both_blocks, pair_blocks)  10.7 us
    convert_element_type x1, local copies, waits for them, and re-layouts, cross_spectrum(): (jnp.stack([real_part, imag_part], axis=1) * scale).astype(jnp.bfloat16)  10.5 us
  transfers between devices with their start and end apart: 1, of which 1 were waited for; matrix products, arithmetic and copies ran while one was open for 0% of the time, Pallas kernels for 0%

commit v1 on v0

v1 whole, which is shorter than its diff:
```python
import functools
import math

import jax
import jax.numpy as jnp
from jax import lax
from jax.experimental import pallas as pl
from jax.experimental.pallas import tpu as pltpu
from jax.sharding import PartitionSpec as P

FREQS = 128
BLOCK = 128
SMOOTH = 4
CHUNKS = 2
MESH = pl.DeviceIdType.MESH


def fourier_table(bins, length):
    positions = jnp.arange(length, dtype=jnp.int32)
    numbers = jnp.arange(1, bins + 1, dtype=jnp.int32)
    turns = (numbers[:, None] * positions[None, :] % length).astype(jnp.float32)
    phase = 2.0 * math.pi * turns / length
    taper = 0.5 - 0.5 * jnp.cos(2.0 * math.pi * positions.astype(jnp.float32) / length)
    table = jnp.stack([taper[None, :] * jnp.cos(phase), -taper[None, :] * jnp.sin(phase)], axis=0)
    return table.astype(jnp.bfloat16).reshape(2 * bins, length)


def radices(n):
    out = []
    while n > 1:
        r = 4 if n % 4 == 0 else (2 if n % 2 == 0 else n)
        out.append(r)
        n //= r
    return out


def split3(x):
    hi = x.astype(jnp.bfloat16)
    rest = x - hi.astype(jnp.float32)
    mid = rest.astype(jnp.bfloat16)
    lo = (rest - mid.astype(jnp.float32)).astype(jnp.bfloat16)
    return hi, mid, lo


NT = (((1,), (1,)), ((), ()))


def exchange_kernel(n, steps, pairs_ref, x_ref, table_ref, owned_ref, spec, sums, gather, wide, send,
                    ssum, rsum, ssem, rsem, ssem2, rsem2, *bufs):
    recv, stage = bufs[:CHUNKS], bufs[CHUNKS:]
    windows, chans, length = x_ref.shape
    freqs = table_ref.shape[0] // 2
    per = windows // CHUNKS
    rows = 2 * per
    me = lax.axis_index("chan")

    barrier = pltpu.get_barrier_semaphore()

    def greet(k, c):
        pl.semaphore_signal(barrier, inc=1, device_id={"chan": lax.rem(me + k, n)}, device_id_type=MESH)
        return c

    lax.fori_loop(1, n, greet, 0)

    which = lax.broadcasted_iota(jnp.int32, (windows, windows * chans), 1) // chans
    mine = lax.broadcasted_iota(jnp.int32, (windows, windows * chans), 0)
    pick = (which == mine).astype(jnp.float32).astype(jnp.bfloat16)
    sums[0] = jnp.dot(
        pick, x_ref[...].reshape(windows * chans, length), preferred_element_type=jnp.float32
    )
    pl.semaphore_wait(barrier, n - 1)

    def sum_copy(phase, stride, radix, j):
        digit = lax.rem(me // stride, radix)
        other = me + (lax.rem(digit + j, radix) - digit) * stride
        return pltpu.make_async_remote_copy(
            src_ref=sums.at[phase], dst_ref=gather.at[phase, j - 1],
            send_sem=ssum.at[phase, j - 1], recv_sem=rsum.at[phase, j - 1],
            device_id={"chan": other}, device_id_type=MESH)

    pending = []
    stride = 1
    for phase, radix in enumerate(steps):
        copies = [sum_copy(phase, stride, radix, j) for j in range(1, radix)]
        for copy in copies:
            copy.start()
        if phase == 0:
            for w in range(windows):
                spec[w] = lax.dot_general(
                    table_ref[...], x_ref[w], NT, preferred_element_type=jnp.float32)
        total = sums[phase]
        for j, copy in enumerate(copies):
            copy.wait_recv()
            total = total + gather[phase, j]
        sums[phase + 1] = total
        pending += copies
        stride *= radix
    mean = sums[len(steps)] / (chans * n)
    common = sum(
        lax.dot_general(table_ref[...], part, NT, preferred_element_type=jnp.float32)
        for part in reversed(split3(mean)))

    fi = lax.broadcasted_iota(jnp.int32, (freqs, freqs), 0)
    gi = lax.broadcasted_iota(jnp.int32, (freqs, freqs), 1)
    near = (jnp.abs(fi - gi) <= SMOOTH).astype(jnp.float32)
    weight = 1.0 / jnp.sum(near, axis=1, keepdims=True)
    near = near.astype(jnp.bfloat16)

    for chunk in range(CHUNKS):
        for v in range(per):
            w = chunk * per + v
            part = spec[w] - common[:, w:w + 1]
            re, im = part[:freqs], part[freqs:]
            amplitude = jnp.sqrt(re * re + im * im)
            hi = amplitude.astype(jnp.bfloat16)
            lo = (amplitude - hi.astype(jnp.float32)).astype(jnp.bfloat16)
            smoothed = (jnp.dot(near, hi, preferred_element_type=jnp.float32)
                        + jnp.dot(near, lo, preferred_element_type=jnp.float32)) * weight
            level = jnp.sum(amplitude, axis=0, keepdims=True) * (1.0 / freqs)
            scale = 1.0 / (smoothed + (0.05 * level + 1e-06))
            wide[chunk, pl.ds(v, freqs, stride=rows), :] = re * scale
            wide[chunk, pl.ds(per + v, freqs, stride=rows), :] = im * scale
        send[chunk] = wide[chunk].astype(jnp.bfloat16).reshape(send.shape[1:])

        def give(k, c, chunk=chunk):
            to = lax.rem(me + k, n)
            pltpu.make_async_remote_copy(
                src_ref=send.at[chunk, to], dst_ref=recv[chunk].at[me],
                send_sem=ssem.at[chunk], recv_sem=rsem.at[chunk],
                device_id={"chan": to}, device_id_type=MESH).start()
            return c

        lax.fori_loop(1, n, give, 0)
        recv[chunk][me] = send[chunk, me]

    def all_of(ref, sem):
        piece = ref.at[pl.ds(0, n - 1)]
        return pltpu.make_async_copy(piece, piece, sem)

    for chunk in range(CHUNKS):
        all_of(recv[chunk], rsem.at[chunk]).wait()

        def route(k, c, chunk=chunk):
            to = lax.rem(me + k, n)
            stage[chunk][to, 0] = recv[chunk][pairs_ref[to, 0]]
            stage[chunk][to, 1] = recv[chunk][pairs_ref[to, 1]]
            pltpu.make_async_remote_copy(
                src_ref=stage[chunk].at[to], dst_ref=owned_ref.at[chunk, me],
                send_sem=ssem2.at[chunk], recv_sem=rsem2.at[chunk],
                device_id={"chan": to}, device_id_type=MESH).start()
            return c

        lax.fori_loop(1, n, route, 0)
        owned_ref[chunk, me, 0] = recv[chunk][pairs_ref[me, 0]]
        owned_ref[chunk, me, 1] = recv[chunk][pairs_ref[me, 1]]

    for copy in pending:
        copy.wait_send()
    for chunk in range(CHUNKS):
        all_of(recv[chunk], ssem.at[chunk]).wait()
        all_of(stage[chunk], ssem2.at[chunk]).wait()
        all_of(stage[chunk], rsem2.at[chunk]).wait()


def exchange(x, pair_blocks, table, n):
    windows, chans, length = x.shape
    freqs = table.shape[0] // 2
    bins = freqs // n
    rows = 2 * windows // CHUNKS
    steps = radices(n)
    most = max(steps) - 1
    piece = (bins, rows, chans)
    bf, f32 = jnp.bfloat16, jnp.float32
    vmem = pl.BlockSpec(memory_space=pltpu.VMEM)
    dma = pltpu.SemaphoreType.DMA
    return pl.pallas_call(
        functools.partial(exchange_kernel, n, steps),
        out_shape=jax.ShapeDtypeStruct((CHUNKS, n, 2) + piece, bf),
        in_specs=[pl.BlockSpec(memory_space=pltpu.SMEM), vmem, vmem],
        out_specs=vmem,
        scratch_shapes=[
            pltpu.VMEM((windows, 2 * freqs, chans), f32),
            pltpu.VMEM((len(steps) + 1, windows, length), f32),
            pltpu.VMEM((len(steps), most, windows, length), f32),
            pltpu.VMEM((CHUNKS, freqs * rows, chans), f32),
            pltpu.VMEM((CHUNKS, n) + piece, bf),
            dma((len(steps), most)), dma((len(steps), most)),
            dma((CHUNKS,)), dma((CHUNKS,)), dma((CHUNKS,)), dma((CHUNKS,)),
        ]
        + [pltpu.VMEM((n,) + piece, bf) for _ in range(CHUNKS)]
        + [pltpu.VMEM((n, 2) + piece, bf) for _ in range(CHUNKS)],
        compiler_params=pltpu.CompilerParams(
            collective_id=0, has_side_effects=True, vmem_limit_bytes=48 * 1024 * 1024),
    )(pair_blocks, x, table)


def cross_kernel(scale, owned_ref, out_ref):
    chunks, group, _, bins, rows, chans = owned_ref.shape
    half = rows // 2
    for s in range(group):
        for f in range(bins):
            first = [owned_ref[c, s, 0, f] for c in range(chunks)]
            turned = []
            for block in first:
                wide = block.astype(jnp.float32)
                turned.append(jnp.concatenate([wide[half:], -wide[:half]], axis=0).astype(jnp.bfloat16))
            left = jnp.concatenate(
                [jnp.concatenate(first, axis=0), jnp.concatenate(turned, axis=0)], axis=1)
            right = jnp.concatenate([owned_ref[c, s, 1, f] for c in range(chunks)], axis=0)
            product = lax.dot_general(
                left, right, (((0,), (0,)), ((), ())), preferred_element_type=jnp.float32) * scale
            out_ref[0, s * bins + f] = product.reshape(2, chans, chans).astype(jnp.bfloat16)


def cross_spectra(owned, freqs, scale):
    chunks, n, two, bins, rows, chans = owned.shape
    group = max(1, 8 // bins)
    return pl.pallas_call(
        functools.partial(cross_kernel, scale),
        grid=(n // group,),
        out_shape=jax.ShapeDtypeStruct((1, freqs, 2, chans, chans), jnp.bfloat16),
        in_specs=[pl.BlockSpec((chunks, group, two, bins, rows, chans), lambda i: (0, i, 0, 0, 0, 0))],
        out_specs=pl.BlockSpec((1, group * bins, 2, chans, chans), lambda i: (0, i, 0, 0, 0)),
        compiler_params=pltpu.CompilerParams(vmem_limit_bytes=32 * 1024 * 1024),
    )(owned)


def shards(samples, pair_blocks):
    windows, length = samples.shape[1:]
    n = lax.axis_size("chan")
    table = fourier_table(FREQS, length)
    owned = exchange(jnp.swapaxes(samples, 0, 1), pair_blocks, table, n)
    return cross_spectra(owned, FREQS, 1.0 / math.sqrt(windows))


def solution(mesh):
    placed = (P(("parts", "chan"), None, None), P("parts", None))
    return jax.shard_map(
        shards,
        mesh=mesh,
        in_specs=placed,
        out_specs=P(("parts", "chan"), None, None, None, None),
        check_vma=False,
    )
```

time: 254 us -> 96.2 us (0.38); the launches traced: 251 us -> 96 us
  blocking collectives: 109 us -> 0 us
  Pallas kernels: 0 us -> 91.2 us
  other arithmetic: 42.9 us -> 1.31 us
  waiting for transfers between devices: 23.9 us -> 0 us
  local copies, waits for them, and re-layouts: 27 us -> 3.51 us
  loops' own time: 20.6 us -> 0 us
  matrix products: 18.8 us -> 0 us
  starting transfers between devices: 8.54 us -> 0 us
    pallas_call x0 -> x2, Pallas kernels: none -> 91.2 us  [the longest x1 81.5 us: exchange(): pl.pallas_call(functools.partial(exchange_kernel, n, steps), out_shape=ja...]
    psum x1 -> x0, blocking collectives: 57 us -> none  [shards(): total = lax.psum(jnp.sum(spectra, axis=3), 'chan')]
    all_to_all x1 -> x0, blocking collectives: 52.4 us -> none  [shards(): lax.all_to_all(stacked, 'chan', split_axis=0, concat_axis=1, tiled=True)]
    all_to_all x1 -> x0, waiting for transfers between devices: 23.9 us -> none  [shards(): lax.all_to_all(whitened, 'chan', split_axis=0, concat_axis=3, tiled=True)]
    another operation x1 -> x0, loops' own time: 20.6 us -> none  [shards(): stacked = lax.map(both_blocks, pair_blocks)]
    another operation x2, other arithmetic: 20.7 us -> 1.26 us  [the longest x1 19.5 us: cross_spectrum(): jnp.stack([real_part, imag_part], axis=1) * scale]
    dot_general x3 -> x0, matrix products: 18.8 us -> none  [the longest x1 13.1 us: cross_spectrum(): lax.dot_general(first, second, (((1,), (1,)), ((0,), (0,))), preferred_el...]
    convert_element_type x2 -> x0, local copies, waits for them, and re-layouts: 12.2 us -> none  [the longest x1 10.5 us: cross_spectrum(): (jnp.stack([real_part, imag_part], axis=1) * scale).astype(jnp.bfloat16)]
  transfers between devices with their start and end apart: 1 -> 0, of which waited for: 1 -> 0; matrix products, arithmetic and copies ran while one was open for 0% -> 0% of each run, Pallas kernels for 0% -> 0%
where the time goes in v1:
time: 96.2 us; the launch traced here: 96 us
  Pallas kernels  91.2 us (95%)
  local copies, waits for them, and re-layouts  3.51 us (4%)
  other arithmetic  1.31 us (1%)
    pallas_call x1, Pallas kernels, exchange(): pl.pallas_call(functools.partial(exchange_kernel, n, steps), out_shape=ja...  81.5 us
    pallas_call x1, Pallas kernels, cross_spectra(): pl.pallas_call(functools.partial(cross_kernel, scale), grid=(n // group,)...  9.64 us
    unnamed x2, local copies, waits for them, and re-layouts  3.51 us

profile of v1, /device:TPU:27, one launch (start us, length us, event | category | flops | bytes accessed | tf_op | source)
XLA Modules:
  0.0 96.0 jit_solution(9649483747377247168)
XLA Ops:
  0.1 0.8 copy.4.pairs_ref
  0.8 1.2 %multiply_convert_fusion.1 = (bf16[1,128,512]{2,1,0:T(8,128)(2,1)S(1)}, bf16[1,128,512]{2,1,0:T(8,128)(2,1)S(1)}) fusion(s32[128]{0:T(128)S(1)} %iota_add_fusion, f32[512]{0:T(512)S(1)} %get-tuple-element.7, f32[512]{0:T(512)S(1)} %get-tuple-element.8), kind=kLoop, calls=%fused_computation.9 | loop fusion | flops 1179648 | bytes 266752 | tf_op jit(solution)/shard_map/convert
  2.1 2.8 %copy.6 = bf16[128,16,512]{2,0,1:T(8,128)(2,1)S(1)} copy(bf16[128,16,512]{2,1,0:T(8,128)(2,1)} %param.2) | data formatting | bytes 4194304 | tf_op args[0]
  4.8 81.5 %shard_map.28.owned_ref = bf16[2,16,2,8,16,128]{5,4,3,2,1,0:T(8,128)(2,1)S(1)} custom-call(s32[16,2]{1,0:T(8,128)S(1)} %copy.4.pairs_ref, bf16[16,128,512]{2,1,0:T(8,128)(2,1)S(1)} %bitcast.4, bf16[256,512]{1,0:T(8,128)(2,1)S(1)} %bitcast.5), custom_call_target="tpu_custom_call" | custom-call | tf_op jit(solution)/shard_map/pallas_call | solution.py:176
  86.4 9.6 %shard_map.29 = bf16[1,128,2,128,128]{4,3,2,1,0:T(8,128)(2,1)} custom-call(bf16[2,16,2,8,16,128]{5,4,3,2,1,0:T(8,128)(2,1)S(1)} %shard_map.28.owned_ref), custom_call_target="tpu_custom_call" | custom-call | tf_op jit(solution)/shard_map/pallas_call | solution.py:218
  (3 shorter events, 0.1 us)

commit v2 on v1

v2 whole, which is shorter than its diff:
```python
import functools
import math

import jax
import jax.numpy as jnp
from jax import lax
from jax.experimental import pallas as pl
from jax.experimental.pallas import tpu as pltpu
from jax.sharding import PartitionSpec as P

FREQS = 128
BLOCK = 128
SMOOTH = 4
CHUNKS = 4
MESH = pl.DeviceIdType.MESH


def fourier_table(bins, length):
    positions = jnp.arange(length, dtype=jnp.int32)
    numbers = jnp.arange(1, bins + 1, dtype=jnp.int32)
    turns = (numbers[:, None] * positions[None, :] % length).astype(jnp.float32)
    phase = 2.0 * math.pi * turns / length
    taper = 0.5 - 0.5 * jnp.cos(2.0 * math.pi * positions.astype(jnp.float32) / length)
    table = jnp.stack([taper[None, :] * jnp.cos(phase), -taper[None, :] * jnp.sin(phase)], axis=0)
    return table.astype(jnp.bfloat16).reshape(2 * bins, length)


def radices(n):
    out = []
    while n > 1:
        r = 4 if n % 4 == 0 else (2 if n % 2 == 0 else n)
        out.append(r)
        n //= r
    return out


def split3(x):
    hi = x.astype(jnp.bfloat16)
    rest = x - hi.astype(jnp.float32)
    mid = rest.astype(jnp.bfloat16)
    lo = (rest - mid.astype(jnp.float32)).astype(jnp.bfloat16)
    return hi, mid, lo


NT = (((1,), (1,)), ((), ()))


def exchange_kernel(n, copies_held, chunks, steps, pairs_ref, x_ref, table_ref, owned_ref, spec, sums, gather, wide, send,
                    ssum, rsum, ssem, rsem, ssem2, rsem2, *bufs):
    recv, stage = bufs[:chunks], bufs[chunks:]
    holders = n // copies_held
    windows, chans, length = x_ref.shape
    freqs = table_ref.shape[0] // 2
    me = lax.axis_index("chan")
    place = lax.rem(me, holders)
    base = me - place

    barrier = pltpu.get_barrier_semaphore()

    def greet(k, c):
        pl.semaphore_signal(barrier, inc=1, device_id={"chan": lax.rem(me + k, n)}, device_id_type=MESH)
        return c

    lax.fori_loop(1, n, greet, 0)

    which = lax.broadcasted_iota(jnp.int32, (windows, windows * chans), 1) // chans
    mine = lax.broadcasted_iota(jnp.int32, (windows, windows * chans), 0)
    pick = (which == mine).astype(jnp.float32).astype(jnp.bfloat16)
    sums[0] = jnp.dot(
        pick, x_ref[...].reshape(windows * chans, length), preferred_element_type=jnp.float32
    )
    pl.semaphore_wait(barrier, n - 1)

    def sum_copy(phase, stride, radix, j):
        digit = lax.rem(me // stride, radix)
        other = me + (lax.rem(digit + j, radix) - digit) * stride
        return pltpu.make_async_remote_copy(
            src_ref=sums.at[phase], dst_ref=gather.at[phase, j - 1],
            send_sem=ssum.at[phase, j - 1], recv_sem=rsum.at[phase, j - 1],
            device_id={"chan": other}, device_id_type=MESH)

    pending = []
    stride = 1
    for phase, radix in enumerate(steps):
        copies = [sum_copy(phase, stride, radix, j) for j in range(1, radix)]
        for copy in copies:
            copy.start()
        if phase == 0:
            for w in range(windows):
                spec[w] = lax.dot_general(
                    table_ref[...], x_ref[w], NT, preferred_element_type=jnp.float32)
        total = sums[phase]
        for j, copy in enumerate(copies):
            copy.wait_recv()
            total = total + gather[phase, j]
        sums[phase + 1] = total
        pending += copies
        stride *= radix
    mean = sums[len(steps)] / (chans * n)
    common = sum(
        lax.dot_general(table_ref[...], part, NT, preferred_element_type=jnp.float32)
        for part in reversed(split3(mean)))

    fi = lax.broadcasted_iota(jnp.int32, (freqs, freqs), 0)
    gi = lax.broadcasted_iota(jnp.int32, (freqs, freqs), 1)
    near = (jnp.abs(fi - gi) <= SMOOTH).astype(jnp.float32)
    weight = 1.0 / jnp.sum(near, axis=1, keepdims=True)
    near = near.astype(jnp.bfloat16)

    for w in range(windows):
        part = spec[w] - common[:, w:w + 1]
        re, im = part[:freqs], part[freqs:]
        amplitude = jnp.sqrt(re * re + im * im)
        hi = amplitude.astype(jnp.bfloat16)
        lo = (amplitude - hi.astype(jnp.float32)).astype(jnp.bfloat16)
        smoothed = (jnp.dot(near, hi, preferred_element_type=jnp.float32)
                    + jnp.dot(near, lo, preferred_element_type=jnp.float32)) * weight
        level = jnp.sum(amplitude, axis=0, keepdims=True) * (1.0 / freqs)
        scale = 1.0 / (smoothed + (0.05 * level + 1e-06))
        wide[pl.ds(w, freqs, stride=2 * windows), :] = re * scale
        wide[pl.ds(windows + w, freqs, stride=2 * windows), :] = im * scale
    send[...] = wide[...].astype(jnp.bfloat16).reshape(send.shape)

    for chunk in range(chunks):

        def give(k, c, chunk=chunk):
            to = lax.rem(me + n // 2 + k, n)

            @pl.when(to != me)
            def _():
                pltpu.make_async_remote_copy(
                    src_ref=send.at[lax.rem(to, holders), chunk], dst_ref=recv[chunk].at[me],
                    send_sem=ssem.at[chunk], recv_sem=rsem.at[chunk],
                    device_id={"chan": to}, device_id_type=MESH).start()

            return c

        lax.fori_loop(0, n, give, 0)
        recv[chunk][me] = send[place, chunk]

    def all_of(ref, sem, count):
        piece = ref.at[pl.ds(0, count)]
        return pltpu.make_async_copy(piece, piece, sem)

    for chunk in range(chunks):
        all_of(recv[chunk], rsem.at[chunk], n - 1).wait()

        def route(k, c, chunk=chunk):
            spot = lax.rem(place + k, holders)
            to = base + spot
            stage[chunk][spot, 0] = recv[chunk][pairs_ref[to, 0]]
            stage[chunk][spot, 1] = recv[chunk][pairs_ref[to, 1]]
            pltpu.make_async_remote_copy(
                src_ref=stage[chunk].at[spot], dst_ref=owned_ref.at[chunk, place],
                send_sem=ssem2.at[chunk], recv_sem=rsem2.at[chunk],
                device_id={"chan": to}, device_id_type=MESH).start()
            return c

        lax.fori_loop(1, holders, route, 0)
        owned_ref[chunk, place, 0] = recv[chunk][pairs_ref[me, 0]]
        owned_ref[chunk, place, 1] = recv[chunk][pairs_ref[me, 1]]

    for copy in pending:
        copy.wait_send()
    for chunk in range(chunks):
        all_of(recv[chunk], ssem.at[chunk], n - 1).wait()
        all_of(stage[chunk], ssem2.at[chunk], holders - 1).wait()
        all_of(stage[chunk], rsem2.at[chunk], holders - 1).wait()


def exchange(x, pair_blocks, table, n):
    windows, chans, length = x.shape
    freqs = table.shape[0] // 2
    copies_held = 2 if n % 2 == 0 and n > 2 else 1
    holders = n // copies_held
    chunks = min(CHUNKS, freqs // holders)
    steps = radices(n)
    most = max(steps) - 1
    piece = (freqs // holders // chunks, 2 * windows, chans)
    bf, f32 = jnp.bfloat16, jnp.float32
    vmem = pl.BlockSpec(memory_space=pltpu.VMEM)
    dma = pltpu.SemaphoreType.DMA
    return pl.pallas_call(
        functools.partial(exchange_kernel, n, copies_held, chunks, steps),
        out_shape=jax.ShapeDtypeStruct((chunks, holders, 2) + piece, bf),
        in_specs=[pl.BlockSpec(memory_space=pltpu.SMEM), vmem, vmem],
        out_specs=vmem,
        scratch_shapes=[
            pltpu.VMEM((windows, 2 * freqs, chans), f32),
            pltpu.VMEM((len(steps) + 1, windows, length), f32),
            pltpu.VMEM((len(steps), most, windows, length), f32),
            pltpu.VMEM((freqs * 2 * windows, chans), f32),
            pltpu.VMEM((holders, chunks) + piece, bf),
            dma((len(steps), most)), dma((len(steps), most)),
            dma((chunks,)), dma((chunks,)), dma((chunks,)), dma((chunks,)),
        ]
        + [pltpu.VMEM((n,) + piece, bf) for _ in range(chunks)]
        + [pltpu.VMEM((holders, 2) + piece, bf) for _ in range(chunks)],
        compiler_params=pltpu.CompilerParams(
            collective_id=0, has_side_effects=True, vmem_limit_bytes=48 * 1024 * 1024),
    )(pair_blocks, x, table)


def cross_kernel(scale, owned_ref, out_ref):
    chunks, group, _, bins, rows, chans = owned_ref.shape
    half = rows // 2
    for s in range(group):
        for c in range(chunks):
            for f in range(bins):
                first, second = owned_ref[c, s, 0, f], owned_ref[c, s, 1, f]
                turned = jnp.concatenate([-second[half:], second[:half]], axis=0)
                product = lax.dot_general(
                    first, jnp.concatenate([second, turned], axis=1),
                    (((0,), (0,)), ((), ())), preferred_element_type=jnp.float32)
                product = (product * scale).astype(jnp.bfloat16)
                at = (s * chunks + c) * bins + f
                out_ref[0, at, 0] = product[:, :chans]
                out_ref[0, at, 1] = product[:, chans:]


def cross_spectra(owned, freqs, scale):
    chunks, n, two, bins, rows, chans = owned.shape
    group = max(1, 8 // (bins * chunks))
    return pl.pallas_call(
        functools.partial(cross_kernel, scale),
        grid=(n // group,),
        out_shape=jax.ShapeDtypeStruct((1, freqs, 2, chans, chans), jnp.bfloat16),
        in_specs=[pl.BlockSpec((chunks, group, two, bins, rows, chans), lambda i: (0, i, 0, 0, 0, 0))],
        out_specs=pl.BlockSpec((1, group * bins * chunks, 2, chans, chans), lambda i: (0, i, 0, 0, 0)),
        compiler_params=pltpu.CompilerParams(vmem_limit_bytes=32 * 1024 * 1024),
    )(owned)


def shards(samples, pair_blocks):
    windows, length = samples.shape[1:]
    n = lax.axis_size("chan")
    table = fourier_table(FREQS, length)
    owned = exchange(jnp.swapaxes(samples, 0, 1), pair_blocks, table, n)
    return cross_spectra(owned, FREQS, 1.0 / math.sqrt(windows))


def solution(mesh):
    placed = (P(("parts", "chan"), None, None), P("parts", None))
    return jax.shard_map(
        shards,
        mesh=mesh,
        in_specs=placed,
        out_specs=P(("parts", "chan"), None, None, None, None),
        check_vma=False,
    )
```

time: 96.2 us -> 84.8 us (0.88); the launches traced: 96 us -> 83.6 us
  Pallas kernels: 91.2 us -> 78.8 us
    pallas_call x1, Pallas kernels: 81.5 us -> 72.4 us  [exchange(): pl.pallas_call(functools.partial(exchange_kernel, n, copies_held, chunks,...]
    pallas_call x1, Pallas kernels: 9.64 us -> 6.39 us  [cross_spectra(): pl.pallas_call(functools.partial(cross_kernel, scale), grid=(n // group,)...]
where the time goes in v2:
time: 84.8 us; the launch traced here: 83.6 us
  Pallas kernels  78.8 us (93%)
  local copies, waits for them, and re-layouts  3.51 us (4%)
  other arithmetic  1.31 us (2%)
    pallas_call x1, Pallas kernels, exchange(): pl.pallas_call(functools.partial(exchange_kernel, n, copies_held, chunks,...  72.4 us
    pallas_call x1, Pallas kernels, cross_spectra(): pl.pallas_call(functools.partial(cross_kernel, scale), grid=(n // group,)...  6.39 us
    unnamed x2, local copies, waits for them, and re-layouts  3.51 us

profile of v2, /device:TPU:27, one launch (start us, length us, event | category | flops | bytes accessed | tf_op | source)
XLA Modules:
  0.0 83.6 jit_solution(2014983025451795018)
XLA Ops:
  0.1 0.8 copy.4.pairs_ref
  0.8 1.2 %multiply_convert_fusion.1 = (bf16[1,128,512]{2,1,0:T(8,128)(2,1)S(1)}, bf16[1,128,512]{2,1,0:T(8,128)(2,1)S(1)}) fusion(s32[128]{0:T(128)S(1)} %iota_add_fusion, f32[512]{0:T(512)S(1)} %get-tuple-element.7, f32[512]{0:T(512)S(1)} %get-tuple-element.8), kind=kLoop, calls=%fused_computation.9 | loop fusion | flops 1179648 | bytes 266752 | tf_op jit(solution)/shard_map/convert
  2.1 2.8 %copy.6 = bf16[128,16,512]{2,0,1:T(8,128)(2,1)S(1)} copy(bf16[128,16,512]{2,1,0:T(8,128)(2,1)} %param.2) | data formatting | bytes 4194304 | tf_op args[0]
  4.8 72.4 %shard_map.28.owned_ref = bf16[4,8,2,4,32,128]{5,4,3,2,1,0:T(8,128)(2,1)S(1)} custom-call(s32[16,2]{1,0:T(8,128)S(1)} %copy.4.pairs_ref, bf16[16,128,512]{2,1,0:T(8,128)(2,1)S(1)} %bitcast.4, bf16[256,512]{1,0:T(8,128)(2,1)S(1)} %bitcast.5), custom_call_target="tpu_custom_call" | custom-call | tf_op jit(solution)/shard_map/pallas_call | solution.py:183
  77.2 6.4 %shard_map.29 = bf16[1,128,2,128,128]{4,3,2,1,0:T(8,128)(2,1)} custom-call(bf16[4,8,2,4,32,128]{5,4,3,2,1,0:T(8,128)(2,1)S(1)} %shard_map.28.owned_ref), custom_call_target="tpu_custom_call" | custom-call | tf_op jit(solution)/shard_map/pallas_call | solution.py:224
  (3 shorter events, 0.1 us)

commit v3 on v2

--- a/solution.py
+++ b/solution.py
@@ -3,6 +3,8 @@
 
 import jax
 import jax.numpy as jnp
+import ml_dtypes
+import numpy as np
 from jax import lax
 from jax.experimental import pallas as pl
 from jax.experimental.pallas import tpu as pltpu
@@ -16,13 +18,12 @@
 
 
 def fourier_table(bins, length):
-    positions = jnp.arange(length, dtype=jnp.int32)
-    numbers = jnp.arange(1, bins + 1, dtype=jnp.int32)
-    turns = (numbers[:, None] * positions[None, :] % length).astype(jnp.float32)
-    phase = 2.0 * math.pi * turns / length
-    taper = 0.5 - 0.5 * jnp.cos(2.0 * math.pi * positions.astype(jnp.float32) / length)
-    table = jnp.stack([taper[None, :] * jnp.cos(phase), -taper[None, :] * jnp.sin(phase)], axis=0)
-    return table.astype(jnp.bfloat16).reshape(2 * bins, length)
+    positions = np.arange(length)
+    turns = np.arange(1, bins + 1)[:, None] * positions[None, :] % length
+    phase = 2.0 * np.pi * turns / length
+    taper = 0.5 - 0.5 * np.cos(2.0 * np.pi * positions / length)
+    table = np.concatenate([taper * np.cos(phase), -taper * np.sin(phase)], axis=0)
+    return jnp.asarray(table.astype(np.float32).astype(ml_dtypes.bfloat16))
 
 
 def radices(n):
@@ -45,16 +46,21 @@
 NT = (((1,), (1,)), ((), ()))
 
 
-def exchange_kernel(n, copies_held, chunks, steps, pairs_ref, x_ref, table_ref, owned_ref, spec, sums, gather, wide, send,
-                    ssum, rsum, ssem, rsem, ssem2, rsem2, *bufs):
+def exchange_kernel(n, copies_held, chunks, steps, pairs_hbm, x_hbm, table_ref, owned_ref, pairs_ref, x_ref,
+                    turned, spec, sums, gather, wide, send,
+                    load, own, ssum, rsum, ssem, rsem, ssem2, rsem2, *bufs):
     recv, stage = bufs[:chunks], bufs[chunks:]
     holders = n // copies_held
-    windows, chans, length = x_ref.shape
+    chans, windows, length = x_ref.shape
     freqs = table_ref.shape[0] // 2
     me = lax.axis_index("chan")
     place = lax.rem(me, holders)
     base = me - place
 
+    fetch = pltpu.make_async_copy(x_hbm, x_ref, load.at[0])
+    fetch.start()
+    fetch_pairs = pltpu.make_async_copy(pairs_hbm, pairs_ref, load.at[1])
+    fetch_pairs.start()
     barrier = pltpu.get_barrier_semaphore()
 
     def greet(k, c):
@@ -63,9 +69,10 @@
 
     lax.fori_loop(1, n, greet, 0)
 
-    which = lax.broadcasted_iota(jnp.int32, (windows, windows * chans), 1) // chans
+    which = lax.broadcasted_iota(jnp.int32, (windows, windows * chans), 1) % windows
     mine = lax.broadcasted_iota(jnp.int32, (windows, windows * chans), 0)
     pick = (which == mine).astype(jnp.float32).astype(jnp.bfloat16)
+    fetch.wait()
     sums[0] = jnp.dot(
         pick, x_ref[...].reshape(windows * chans, length), preferred_element_type=jnp.float32
     )
@@ -86,9 +93,13 @@
         for copy in copies:
             copy.start()
         if phase == 0:
-            for w in range(windows):
-                spec[w] = lax.dot_general(
-                    table_ref[...], x_ref[w], NT, preferred_element_type=jnp.float32)
+            turned[...] = jnp.swapaxes(x_ref[...], 0, 1)
+            for w in range(0, windows, 2):
+                both = lax.dot_general(
+                    table_ref[...], turned[w:w + 2].reshape(2 * chans, length), NT,
+                    preferred_element_type=jnp.float32)
+                spec[w] = both[:, :chans]
+                spec[w + 1] = both[:, chans:]
         total = sums[phase]
         for j, copy in enumerate(copies):
             copy.wait_recv()
@@ -138,10 +149,13 @@
         lax.fori_loop(0, n, give, 0)
         recv[chunk][me] = send[place, chunk]
 
+    kept = []
+
     def all_of(ref, sem, count):
         piece = ref.at[pl.ds(0, count)]
         return pltpu.make_async_copy(piece, piece, sem)
 
+    fetch_pairs.wait()
     for chunk in range(chunks):
         all_of(recv[chunk], rsem.at[chunk], n - 1).wait()
 
@@ -157,11 +171,17 @@
             return c
 
         lax.fori_loop(1, holders, route, 0)
-        owned_ref[chunk, place, 0] = recv[chunk][pairs_ref[me, 0]]
-        owned_ref[chunk, place, 1] = recv[chunk][pairs_ref[me, 1]]
+        stage[chunk][place, 0] = recv[chunk][pairs_ref[me, 0]]
+        stage[chunk][place, 1] = recv[chunk][pairs_ref[me, 1]]
+        keep = pltpu.make_async_copy(
+            stage[chunk].at[place], owned_ref.at[chunk, place], own.at[chunk])
+        keep.start()
+        kept.append(keep)
 
     for copy in pending:
         copy.wait_send()
+    for copy in kept:
+        copy.wait()
     for chunk in range(chunks):
         all_of(recv[chunk], ssem.at[chunk], n - 1).wait()
         all_of(stage[chunk], ssem2.at[chunk], holders - 1).wait()
@@ -169,7 +189,7 @@
 
 
 def exchange(x, pair_blocks, table, n):
-    windows, chans, length = x.shape
+    chans, windows, length = x.shape
     freqs = table.shape[0] // 2
     copies_held = 2 if n % 2 == 0 and n > 2 else 1
     holders = n // copies_held
@@ -179,18 +199,23 @@
     piece = (freqs // holders // chunks, 2 * windows, chans)
     bf, f32 = jnp.bfloat16, jnp.float32
     vmem = pl.BlockSpec(memory_space=pltpu.VMEM)
+    anywhere = pl.BlockSpec(memory_space=pl.ANY)
     dma = pltpu.SemaphoreType.DMA
     return pl.pallas_call(
         functools.partial(exchange_kernel, n, copies_held, chunks, steps),
         out_shape=jax.ShapeDtypeStruct((chunks, holders, 2) + piece, bf),
-        in_specs=[pl.BlockSpec(memory_space=pltpu.SMEM), vmem, vmem],
-        out_specs=vmem,
+        in_specs=[anywhere, anywhere, vmem],
+        out_specs=anywhere,
         scratch_shapes=[
+            pltpu.SMEM(pair_blocks.shape, jnp.int32),
+            pltpu.VMEM(x.shape, bf),
+            pltpu.VMEM((windows, chans, length), bf),
             pltpu.VMEM((windows, 2 * freqs, chans), f32),
             pltpu.VMEM((len(steps) + 1, windows, length), f32),
             pltpu.VMEM((len(steps), most, windows, length), f32),
             pltpu.VMEM((freqs * 2 * windows, chans), f32),
             pltpu.VMEM((holders, chunks) + piece, bf),
+            dma((2,)), dma((chunks,)),
             dma((len(steps), most)), dma((len(steps), most)),
             dma((chunks,)), dma((chunks,)), dma((chunks,)), dma((chunks,)),
         ]
@@ -204,15 +229,18 @@
 def cross_kernel(scale, owned_ref, out_ref):
     chunks, group, _, bins, rows, chans = owned_ref.shape
     half = rows // 2
+    exact = math.frexp(scale)[0] == 0.5
     for s in range(group):
         for c in range(chunks):
             for f in range(bins):
                 first, second = owned_ref[c, s, 0, f], owned_ref[c, s, 1, f]
+                if exact:
+                    first = first * jnp.bfloat16(scale)
                 turned = jnp.concatenate([-second[half:], second[:half]], axis=0)
                 product = lax.dot_general(
                     first, jnp.concatenate([second, turned], axis=1),
                     (((0,), (0,)), ((), ())), preferred_element_type=jnp.float32)
-                product = (product * scale).astype(jnp.bfloat16)
+                product = (product if exact else product * scale).astype(jnp.bfloat16)
                 at = (s * chunks + c) * bins + f
                 out_ref[0, at, 0] = product[:, :chans]
                 out_ref[0, at, 1] = product[:, chans:]
@@ -235,7 +263,7 @@
     windows, length = samples.shape[1:]
     n = lax.axis_size("chan")
     table = fourier_table(FREQS, length)
-    owned = exchange(jnp.swapaxes(samples, 0, 1), pair_blocks, table, n)
+    owned = exchange(samples, pair_blocks, table, n)
     return cross_spectra(owned, FREQS, 1.0 / math.sqrt(windows))
 
 

time: 84.8 us -> 82.9 us (0.978)
  other arithmetic: 1.31 us -> 0 us
    another operation x2 -> x0, other arithmetic: 1.26 us -> none
    unnamed x2 -> x5, local copies, waits for them, and re-layouts: 3.51 us -> 3.29 us
where the time goes in v3:
time: 82.9 us; the launch traced here: 81.6 us
  Pallas kernels  78.3 us (94%)
  local copies, waits for them, and re-layouts  3.29 us (4%)
    pallas_call x1, Pallas kernels, exchange(): pl.pallas_call(functools.partial(exchange_kernel, n, copies_held, chunks,...  71.9 us
    pallas_call x1, Pallas kernels, cross_spectra(): pl.pallas_call(functools.partial(cross_kernel, scale), grid=(n // group,)...  6.41 us
    unnamed x5, local copies, waits for them, and re-layouts  3.29 us

profile of v3, /device:TPU:27, one launch (start us, length us, event | category | flops | bytes accessed | tf_op | source)
XLA Modules:
  0.0 81.6 jit_solution(4547470316895544660)
XLA Ops:
  0.0 0.8 copy.4.pairs_hbm
  0.8 0.0 copy-start
  0.8 1.6 %copy-done = bf16[128,16,512]{2,1,0:T(8,128)(2,1)S(1)} copy-done((bf16[128,16,512]{2,1,0:T(8,128)(2,1)S(1)}, bf16[128,16,512]{2,1,0:T(8,128)(2,1)}, u32[]{:S(2)}) %copy-start) | copy-done | bytes 2097176
  2.3 0.0 copy-start.1
  2.3 0.9 %copy-done.1 = bf16[256,512]{1,0:T(8,128)(2,1)S(1)} copy-done((bf16[256,512]{1,0:T(8,128)(2,1)S(1)}, bf16[256,512]{1,0:T(8,128)(2,1)}, u32[]{:S(2)}) %copy-start.1) | copy-done | bytes 262168
  3.3 71.9 %shard_map.37.owned_ref = bf16[4,8,2,4,32,128]{5,4,3,2,1,0:T(8,128)(2,1)S(1)} custom-call(s32[16,2]{1,0:T(8,128)S(1)} %copy.4.pairs_hbm, bf16[128,16,512]{2,1,0:T(8,128)(2,1)S(1)} %copy-done, bf16[256,512]{1,0:T(8,128)(2,1)S(1)} %copy-done.1), custom_call_target="tpu_custom_call" | custom-call | tf_op jit(solution)/shard_map/pallas_call | solution.py:204
  75.2 6.4 %shard_map.38 = bf16[1,128,2,128,128]{4,3,2,1,0:T(8,128)(2,1)} custom-call(bf16[4,8,2,4,32,128]{5,4,3,2,1,0:T(8,128)(2,1)S(1)} %shard_map.37.owned_ref), custom_call_target="tpu_custom_call" | custom-call | tf_op jit(solution)/shard_map/pallas_call | solution.py:252
Async XLA Ops:
  0.8 1.6 %copy-start = (bf16[128,16,512]{2,1,0:T(8,128)(2,1)S(1)}, bf16[128,16,512]{2,1,0:T(8,128)(2,1)}, u32[]{:S(2)}) copy-start(bf16[128,16,512]{2,1,0:T(8,128)(2,1)} %x_hbm.1) | copy-start | bytes 6291460
  2.3 0.9 %copy-start.1 = (bf16[256,512]{1,0:T(8,128)(2,1)S(1)}, bf16[256,512]{1,0:T(8,128)(2,1)}, u32[]{:S(2)}) copy-start(bf16[256,512]{1,0:T(8,128)(2,1)} %constant.2.clone.table_ref) | copy-start | bytes 786436

commit v4 on v3

--- a/solution.py
+++ b/solution.py
@@ -46,8 +46,8 @@
 NT = (((1,), (1,)), ((), ()))
 
 
-def exchange_kernel(n, copies_held, chunks, steps, pairs_hbm, x_hbm, table_ref, owned_ref, pairs_ref, x_ref,
-                    turned, spec, sums, gather, wide, send,
+def exchange_kernel(n, copies_held, chunks, steps, pairs_hbm, x_hbm, table_hbm, owned_ref, pairs_ref, x_ref,
+                    table_ref, turned, spec, sums, gather, wide, send,
                     load, own, ssum, rsum, ssem, rsem, ssem2, rsem2, *bufs):
     recv, stage = bufs[:chunks], bufs[chunks:]
     holders = n // copies_held
@@ -61,6 +61,8 @@
     fetch.start()
     fetch_pairs = pltpu.make_async_copy(pairs_hbm, pairs_ref, load.at[1])
     fetch_pairs.start()
+    fetch_table = pltpu.make_async_copy(table_hbm, table_ref, load.at[2])
+    fetch_table.start()
     barrier = pltpu.get_barrier_semaphore()
 
     def greet(k, c):
@@ -73,9 +75,13 @@
     mine = lax.broadcasted_iota(jnp.int32, (windows, windows * chans), 0)
     pick = (which == mine).astype(jnp.float32).astype(jnp.bfloat16)
     fetch.wait()
-    sums[0] = jnp.dot(
+    local = jnp.dot(
         pick, x_ref[...].reshape(windows * chans, length), preferred_element_type=jnp.float32
     )
+    fetch_table.wait()
+    sums[0] = sum(
+        lax.dot_general(part, table_ref[...], NT, preferred_element_type=jnp.float32)
+        for part in reversed(split3(local)))
     pl.semaphore_wait(barrier, n - 1)
 
     def sum_copy(phase, stride, radix, j):
@@ -107,10 +113,7 @@
         sums[phase + 1] = total
         pending += copies
         stride *= radix
-    mean = sums[len(steps)] / (chans * n)
-    common = sum(
-        lax.dot_general(table_ref[...], part, NT, preferred_element_type=jnp.float32)
-        for part in reversed(split3(mean)))
+    common = (sums[len(steps)] / (chans * n)).T
 
     fi = lax.broadcasted_iota(jnp.int32, (freqs, freqs), 0)
     gi = lax.broadcasted_iota(jnp.int32, (freqs, freqs), 1)
@@ -198,31 +201,31 @@
     most = max(steps) - 1
     piece = (freqs // holders // chunks, 2 * windows, chans)
     bf, f32 = jnp.bfloat16, jnp.float32
-    vmem = pl.BlockSpec(memory_space=pltpu.VMEM)
     anywhere = pl.BlockSpec(memory_space=pl.ANY)
     dma = pltpu.SemaphoreType.DMA
     return pl.pallas_call(
         functools.partial(exchange_kernel, n, copies_held, chunks, steps),
         out_shape=jax.ShapeDtypeStruct((chunks, holders, 2) + piece, bf),
-        in_specs=[anywhere, anywhere, vmem],
+        in_specs=[anywhere, anywhere, anywhere],
         out_specs=anywhere,
         scratch_shapes=[
             pltpu.SMEM(pair_blocks.shape, jnp.int32),
             pltpu.VMEM(x.shape, bf),
+            pltpu.VMEM(table.shape, bf),
             pltpu.VMEM((windows, chans, length), bf),
             pltpu.VMEM((windows, 2 * freqs, chans), f32),
-            pltpu.VMEM((len(steps) + 1, windows, length), f32),
-            pltpu.VMEM((len(steps), most, windows, length), f32),
+            pltpu.VMEM((len(steps) + 1, windows, 2 * freqs), f32),
+            pltpu.VMEM((len(steps), most, windows, 2 * freqs), f32),
             pltpu.VMEM((freqs * 2 * windows, chans), f32),
             pltpu.VMEM((holders, chunks) + piece, bf),
-            dma((2,)), dma((chunks,)),
+            dma((3,)), dma((chunks,)),
             dma((len(steps), most)), dma((len(steps), most)),
             dma((chunks,)), dma((chunks,)), dma((chunks,)), dma((chunks,)),
         ]
         + [pltpu.VMEM((n,) + piece, bf) for _ in range(chunks)]
         + [pltpu.VMEM((holders, 2) + piece, bf) for _ in range(chunks)],
         compiler_params=pltpu.CompilerParams(
-            collective_id=0, has_side_effects=True, vmem_limit_bytes=48 * 1024 * 1024),
+            collective_id=0, has_side_effects=True, vmem_limit_bytes=60 * 1024 * 1024),
     )(pair_blocks, x, table)
 
 
@@ -255,7 +258,7 @@
         out_shape=jax.ShapeDtypeStruct((1, freqs, 2, chans, chans), jnp.bfloat16),
         in_specs=[pl.BlockSpec((chunks, group, two, bins, rows, chans), lambda i: (0, i, 0, 0, 0, 0))],
         out_specs=pl.BlockSpec((1, group * bins * chunks, 2, chans, chans), lambda i: (0, i, 0, 0, 0)),
-        compiler_params=pltpu.CompilerParams(vmem_limit_bytes=32 * 1024 * 1024),
+        compiler_params=pltpu.CompilerParams(vmem_limit_bytes=60 * 1024 * 1024),
     )(owned)
 
 

time: 82.9 us -> 81.1 us (0.978)
  local copies, waits for them, and re-layouts: 3.29 us -> 1.35 us
    unnamed x5 -> x1, local copies, waits for them, and re-layouts: 3.29 us -> 1.35 us
    pallas_call x1, Pallas kernels: 6.41 us -> 8.34 us  [cross_spectra(): pl.pallas_call(functools.partial(cross_kernel, scale), grid=(n // group,)...]
    pallas_call x1, Pallas kernels: 71.9 us -> 70.5 us  [exchange(): pl.pallas_call(functools.partial(exchange_kernel, n, copies_held, chunks,...]
where the time goes in v4:
time: 81.1 us; the launch traced here: 80.2 us
  Pallas kernels  78.8 us (97%)
  local copies, waits for them, and re-layouts  1.35 us (2%)
    pallas_call x1, Pallas kernels, exchange(): pl.pallas_call(functools.partial(exchange_kernel, n, copies_held, chunks,...  70.5 us
    pallas_call x1, Pallas kernels, cross_spectra(): pl.pallas_call(functools.partial(cross_kernel, scale), grid=(n // group,)...  8.34 us

profile of v4, /device:TPU:27, one launch (start us, length us, event | category | flops | bytes accessed | tf_op | source)
XLA Modules:
  0.0 80.2 jit_solution(17611037104428620038)
XLA Ops:
  0.0 1.4 %copy.4.pairs_hbm = s32[16,2]{1,0:T(8,128)} copy(s32[16,2]{0,1:T(2,128)} %param.4) | data formatting | bytes 256 | tf_op args[1]
  1.4 70.5 %shard_map.37.owned_ref = bf16[4,8,2,4,32,128]{5,4,3,2,1,0:T(8,128)(2,1)} custom-call(s32[16,2]{1,0:T(8,128)} %copy.4.pairs_hbm, bf16[128,16,512]{2,1,0:T(8,128)(2,1)} %x_hbm.1, bf16[256,512]{1,0:T(8,128)(2,1)} %constant.2.clone.table_hbm), custom_call_target="tpu_custom_call" | custom-call | tf_op jit(solution)/shard_map/pallas_call | solution.py:206
  71.8 8.3 %shard_map.38 = bf16[1,128,2,128,128]{4,3,2,1,0:T(8,128)(2,1)} custom-call(bf16[4,8,2,4,32,128]{5,4,3,2,1,0:T(8,128)(2,1)} %shard_map.37.owned_ref), custom_call_target="tpu_custom_call" | custom-call | tf_op jit(solution)/shard_map/pallas_call | solution.py:255

commit v5 on v4

--- a/solution.py
+++ b/solution.py
@@ -207,7 +207,7 @@
         functools.partial(exchange_kernel, n, copies_held, chunks, steps),
         out_shape=jax.ShapeDtypeStruct((chunks, holders, 2) + piece, bf),
         in_specs=[anywhere, anywhere, anywhere],
-        out_specs=anywhere,
+        out_specs=pl.BlockSpec(memory_space=pltpu.VMEM),
         scratch_shapes=[
             pltpu.SMEM(pair_blocks.shape, jnp.int32),
             pltpu.VMEM(x.shape, bf),
@@ -258,7 +258,7 @@
         out_shape=jax.ShapeDtypeStruct((1, freqs, 2, chans, chans), jnp.bfloat16),
         in_specs=[pl.BlockSpec((chunks, group, two, bins, rows, chans), lambda i: (0, i, 0, 0, 0, 0))],
         out_specs=pl.BlockSpec((1, group * bins * chunks, 2, chans, chans), lambda i: (0, i, 0, 0, 0)),
-        compiler_params=pltpu.CompilerParams(vmem_limit_bytes=60 * 1024 * 1024),
+        compiler_params=pltpu.CompilerParams(vmem_limit_bytes=32 * 1024 * 1024),
     )(owned)
 
 

time: 81.1 us -> 81.9 us (level)
  local copies, waits for them, and re-layouts: 1.35 us -> 2.94 us
    pallas_call x1, Pallas kernels: 8.34 us -> 6.39 us  [cross_spectra(): pl.pallas_call(functools.partial(cross_kernel, scale), grid=(n // group,)...]
    unnamed x1 -> x3, local copies, waits for them, and re-layouts: 1.35 us -> 2.94 us
    pallas_call x1, Pallas kernels: 70.5 us -> 71.7 us  [exchange(): pl.pallas_call(functools.partial(exchange_kernel, n, copies_held, chunks,...]
where the time goes in v5:
time: 81.9 us; the launch traced here: 81 us
  Pallas kernels  78.1 us (95%)
  local copies, waits for them, and re-layouts  2.94 us (4%)
    pallas_call x1, Pallas kernels, exchange(): pl.pallas_call(functools.partial(exchange_kernel, n, copies_held, chunks,...  71.7 us
    pallas_call x1, Pallas kernels, cross_spectra(): pl.pallas_call(functools.partial(cross_kernel, scale), grid=(n // group,)...  6.39 us
    unnamed x3, local copies, waits for them, and re-layouts  2.94 us

profile of v5, /device:TPU:27, one launch (start us, length us, event | category | flops | bytes accessed | tf_op | source)
XLA Modules:
  0.0 81.0 jit_solution(10307200315485170863)
XLA Ops:
  0.0 1.4 %copy.4.pairs_hbm = s32[16,2]{1,0:T(8,128)} copy(s32[16,2]{0,1:T(2,128)} %param.4) | data formatting | bytes 256 | tf_op args[1]
  1.4 71.7 %shard_map.37.owned_ref = bf16[4,8,2,4,32,128]{5,4,3,2,1,0:T(8,128)(2,1)} custom-call(s32[16,2]{1,0:T(8,128)} %copy.4.pairs_hbm, bf16[128,16,512]{2,1,0:T(8,128)(2,1)} %x_hbm.1, bf16[256,512]{1,0:T(8,128)(2,1)} %constant.2.clone.table_hbm), custom_call_target="tpu_custom_call" | custom-call | tf_op jit(solution)/shard_map/pallas_call | solution.py:206
  73.1 0.0 copy-start
  73.1 1.6 %copy-done = bf16[4,8,2,4,32,128]{5,4,3,2,1,0:T(8,128)(2,1)S(1)} copy-done((bf16[4,8,2,4,32,128]{5,4,3,2,1,0:T(8,128)(2,1)S(1)}, bf16[4,8,2,4,32,128]{5,4,3,2,1,0:T(8,128)(2,1)}, u32[]{:S(2)}) %copy-start) | copy-done | bytes 2097176
  74.7 6.4 %shard_map.38 = bf16[1,128,2,128,128]{4,3,2,1,0:T(8,128)(2,1)} custom-call(bf16[4,8,2,4,32,128]{5,4,3,2,1,0:T(8,128)(2,1)S(1)} %copy-done), custom_call_target="tpu_custom_call" | custom-call | tf_op jit(solution)/shard_map/pallas_call | solution.py:255
Async XLA Ops:
  73.1 1.6 %copy-start = (bf16[4,8,2,4,32,128]{5,4,3,2,1,0:T(8,128)(2,1)S(1)}, bf16[4,8,2,4,32,128]{5,4,3,2,1,0:T(8,128)(2,1)}, u32[]{:S(2)}) copy-start(bf16[4,8,2,4,32,128]{5,4,3,2,1,0:T(8,128)(2,1)} %shard_map.37.owned_ref) | copy-start | bytes 6291460
